TPU v7x, 32 devices: a whole 2x2x4 slice. The times are simulated.
32 devices in a mesh: hyp: 4 (over y, x), row: 2 (over core), col: 4 (over z).
Axes of the slice: x: 2, y: 2, z: 4, core: 2. Of those that a mesh axis runs over, the one named last changes fastest.
Arguments:
- left_factors: bfloat16 [4, 48, 48, 256, 256], P('hyp', 'row', 'col'), may hold values from -0.0546875 to 0.0546875
- right_factors: bfloat16 [4, 48, 48, 256, 256], P('hyp', 'row', 'col'), may hold values from -0.375 to 0.375
- admissible: int32 [48, 48], P('row', 'col'), may hold values from 0 to 1, as said below
- tile_ranks: int32 [4, 48, 48], P('hyp', 'row', 'col'), may hold values from 32 to 256
- probes: bfloat16 [12288, 128], P('col', 'row'), may hold values from -6 to 6
- solved_probes: bfloat16 [12288, 128], P('row', 'col'), may hold values from -180 to 180
- data_terms: float32 [4], P('hyp'), may hold values from -64 to 64
- log_params: float32 [4], replicated, may hold values from -4 to 4
Outputs:
- forward: bfloat16 [4, 12288, 128], P('hyp', 'row', 'col')
- backward: bfloat16 [4, 12288, 128], P('hyp', 'col', 'row')
- new_params: float32 [4], replicated
Inputs may be any that keep to these rules, and one draw needn't show every extreme that they name: `admissible`: Symmetric; diagonal tiles are near field (0); a tile is near field when it lies within a small drawn reach of the diagonal. `tile_ranks`: only read for far-field tiles.
All inputs are finite; a program needn't handle non-finite values.
Results may differ from a plain program's by a relative error of at most 0.0046.
The roundings to bfloat16 on the way count: a program that leaves them out, or rounds other values in their place, can miss the bound.
Values may be sent and summed in bfloat16 or wider, within the bound.
A program may use at most 128 MiB of HBM per device.

v0:
```python
import jax
import jax.numpy as jnp
from jax import lax
from jax.sharding import PartitionSpec as P

step_rate = 0.5


def local(
    left_factors,
    right_factors,
    admissible,
    tile_ranks,
    probes,
    solved_probes,
    data_terms,
    log_params,
):
    left_tiles = left_factors[0]
    right_tiles = right_factors[0]
    row_tiles, col_tiles, leaf_size, rank_cap = left_tiles.shape
    ranks_used = jnp.where(admissible == 0, rank_cap, tile_ranks[0])
    slot_index = lax.broadcasted_iota(jnp.int32, (row_tiles, col_tiles, rank_cap), 2)
    kept_mask = (slot_index < ranks_used[:, :, None]).astype(jnp.float32)
    piece = lax.all_gather(probes, "row", axis=1, tiled=True)
    blocks = piece.reshape(col_tiles, leaf_size, piece.shape[1])
    coefs = jnp.einsum("ijbr,jbp->ijrp", right_tiles, blocks, preferred_element_type=jnp.float32)
    forward_coefs = (coefs * kept_mask[..., None]).astype(jnp.bfloat16)
    forward_part = jnp.einsum(
        "ijbr,ijrp->ibp", left_tiles, forward_coefs, preferred_element_type=jnp.float32
    )
    forward_part = forward_part.reshape(row_tiles * leaf_size, forward_part.shape[2])
    solved_wide = lax.all_gather(solved_probes, "col", axis=1, tiled=True)
    probe_count = solved_wide.shape[1]
    solved_blocks = solved_wide.reshape(row_tiles, leaf_size, probe_count)
    backward_coefs = jnp.einsum(
        "ijbr,ibp->ijrp", left_tiles, solved_blocks, preferred_element_type=jnp.float32
    )
    backward_coefs = (backward_coefs * kept_mask[..., None]).astype(jnp.bfloat16)
    backward_part = jnp.einsum(
        "ijbr,ijrp->jbp", right_tiles, backward_coefs, preferred_element_type=jnp.float32
    )
    backward_part = backward_part.reshape(col_tiles * leaf_size, probe_count)
    forward_sum = lax.psum_scatter(forward_part, "col", scatter_dimension=1, tiled=True)
    backward_sum = lax.psum_scatter(backward_part, "row", scatter_dimension=1, tiled=True)
    local_trace = jnp.sum(solved_probes.astype(jnp.float32) * forward_sum)
    trace_total = lax.psum(local_trace, ("row", "col"))
    trace_value = trace_total / probe_count
    gradient = 0.5 * (data_terms - trace_value)
    gradients = lax.all_gather(gradient, "hyp", axis=0, tiled=True)
    grad_norm = jnp.sqrt(jnp.sum(gradients * gradients))
    new_params = log_params - step_rate * gradients / grad_norm
    return (
        forward_sum.astype(jnp.bfloat16)[None],
        backward_sum.astype(jnp.bfloat16)[None],
        new_params,
    )


def solution(mesh):
    return jax.shard_map(
        local,
        mesh=mesh,
        in_specs=(
            P("hyp", "row", "col", None, None),
            P("hyp", "row", "col", None, None),
            P("row", "col"),
            P("hyp", "row", "col"),
            P("col", "row"),
            P("row", "col"),
            P("hyp"),
            P(),
        ),
        out_specs=(P("hyp", "row", "col"), P("hyp", "col", "row"), P()),
        check_vma=False,
    )
```

profile of v0, /device:TPU:0, one launch (start us, length us, event | category | flops | bytes accessed | tf_op | source)
XLA Modules:
  0.0 165.2 jit_solution(11286835188704644287)
XLA Ops:
  7.2 0.0 all-gather.2.cloned.1.call-start
  7.2 0.7 all-gather.2.cloned.1.call-update
  7.9 0.0 reduce-scatter.7.cloned.1.call-start
  7.9 0.7 bitcast_select_fusion
  8.7 0.1 fusion.32
  8.8 0.0 copy-start.1
  8.8 2.7 %all_gather.9 = bf16[3072,128]{0,1:T(8,128)(2,1)S(1)} all-gather(bf16[3072,64]{0,1:T(8,128)(2,1)} %param.12), channel_id=1, replica_groups=mesh['hyp'=4,'row'=2,'col'=4] {'row'}, dimensions={1}, use_global_device_ids=true | all-gather | bytes 1179648 | tf_op jit(solution)/shard_map/all_gather | solution.py:25
  11.4 0.4 copy.34
  11.8 0.0 copy-done.1
  11.8 29.1 %fusion.20 = f32[24,256,128]{1,2,0:T(8,128)} fusion(f32[24,12,256]{2,0,1:T(8,128)S(1)} %fusion.32, bf16[12,256,128,1]{2,1,3,0:T(8,128)(2,1)S(1)} %bitcast.68, bf16[1,24,12,256,256]{4,3,2,1,0:T(8,128)(2,1)} %param.8, bf16[1,24,12,256,256]{4,3,2,1,0:T(8,128)(2,1)} %param.9), kind=kOutput, calls=%fused_computation.13 | convolution fusion | flops 9682550784 | bytes 79724544 | tf_op jit(solution)/shard_map/ijbr,ijrp->ibp/dot_general | solution.py:29
  41.0 2.4 %copy.38 = f32[24,256,128]{2,1,0:T(8,128)S(1)} copy(f32[24,256,128]{1,2,0:T(8,128)} %fusion.20) | data formatting | bytes 6291456 | tf_op jit(solution)/shard_map/ijbr,ijrp->ibp/dot_general | solution.py:29
  43.3 2.3 %copy.54 = f32[6144,128]{0,1:T(8,128)} copy(f32[6144,128]{1,0:T(8,128)S(1)} %bitcast.60) | data formatting | bytes 6291456
  45.7 0.0 reduce-scatter.7.cloned.1.call-update
  45.7 0.0 reduce-scatter.9.cloned.1.call-start
  45.8 3.6 %all-gather.2.cloned.1.call-done = bf16[6144,128]{0,1:T(8,128)(2,1)} async-done(((bf16[6144,32]{0,1:T(8,128)(2,1)}), bf16[6144,128]{0,1:T(8,128)(2,1)}) %all-gather.2.cloned.1.call-update) | async-done | bytes 1572880 | tf_op jit(solution)/shard_map/all_gather | solution.py:33
  49.4 1.9 %copy.39 = bf16[6144,128]{1,0:T(8,128)(2,1)S(1)} copy(bf16[6144,128]{0,1:T(8,128)(2,1)} %all-gather.2.cloned.1.call-done) | data formatting | bytes 3145728 | tf_op jit(solution)/shard_map/all_gather | solution.py:33
  51.3 0.0 copy-start.3
  51.3 0.0 copy-start
  51.3 0.0 copy-start.2
  51.3 28.0 %fusion.27 = f32[12,256,128]{1,2,0:T(8,128)S(1)} fusion(f32[24,12,256]{2,0,1:T(8,128)} %copy-done.1, bf16[24,256,128,1]{2,1,0,3:T(8,128)(2,1)S(1)} %bitcast.66, bf16[1,24,12,256,256]{4,3,2,1,0:T(8,128)(2,1)} %param.8, bf16[1,24,12,256,256]{4,3,2,1,0:T(8,128)(2,1)} %param.9), kind=kOutput, calls=%fused_computation.15 | convolution fusion | flops 9682550784 | bytes 78938112 | tf_op jit(solution)/shard_map/ijbr,ijrp->jbp/dot_general | solution.py:40
  79.4 0.5 copy.43
  79.9 1.6 copy.56
  81.5 0.0 reduce-scatter.9.cloned.1.call-update
  82.1 0.0 copy-done.3
  82.2 0.6 dynamic-slice
  82.7 28.1 %reduce-scatter.7.cloned.1.call-done = f32[32,6144]{1,0:T(8,128)} async-done(((f32[128,6144]{1,0:T(8,128)}), f32[32,6144]{1,0:T(8,128)}) %reduce-scatter.7.cloned.1.call-update) | async-done | bytes 786448
  110.9 0.0 copy-done
  110.9 1.9 %multiply_reduce_fusion = f32[]{:T(128)} fusion(bf16[6144,32]{0,1:T(8,128)(2,1)S(1)} %copy-done, f32[32,6144]{1,0:T(8,128)} %reduce-scatter.7.cloned.1.call-done), kind=kLoop, calls=%fused_computation.16 | loop fusion | flops 589823 | bytes 1179652 | tf_op jit(solution)/shard_map/reduce_sum | solution.py:46
  112.8 9.4 %reduce-scatter.9.cloned.1.call-done = f32[64,3072]{1,0:T(8,128)} async-done(((f32[128,3072]{1,0:T(8,128)}), f32[64,3072]{1,0:T(8,128)}) %reduce-scatter.9.cloned.1.call-update) | async-done | bytes 786448
  122.2 1.5 copy.57
  123.7 17.8 %psum.7 = f32[]{:T(128)} all-reduce(f32[]{:T(128)} %multiply_reduce_fusion), channel_id=1, replica_groups=mesh['hyp'=4,'row'=2,'col'=4] {'row','col'}, use_global_device_ids=true, to_apply=%region_3.4 | all-reduce | flops 1 | bytes 8 | tf_op jit(solution)/shard_map/psum | solution.py:47
  142.2 0.7 multiply_dynamic-update-slice_fusion
  142.9 1.0 copy.46
  143.9 9.8 %all-reduce = f32[4]{0:T(128)S(1)} all-reduce(f32[4]{0:T(128)S(1)} %multiply_dynamic-update-slice_fusion), channel_id=1, replica_groups=mesh['hyp'=4,'row'=2,'col'=4] {'hyp'}, use_global_device_ids=true, to_apply=%add | all-reduce | flops 4 | bytes 32
  153.8 0.6 multiply_reduce_fusion.1
  155.1 1.8 %copy.55 = bf16[6144,32]{1,0:T(8,128)(2,1)S(1)} copy(f32[6144,32]{0,1:T(8,128)} %bitcast.65) | data formatting | bytes 1179648
  156.8 1.3 copy.45
  158.2 0.0 copy-done.2
  158.2 0.5 divide_subtract_fusion
  (1 shorter events, 0.0 us)
Async XLA Ops:
  7.2 42.2 %all-gather.2.cloned.1.call-start = ((), (), s32[]{:S(2)}) async-start(), calls=%async_computation.2 | async-start | bytes 1966080 | tf_op jit(solution)/shard_map/all_gather | solution.py:33
  7.9 103.0 %reduce-scatter.7.cloned.1.call-start = ((), (), s32[]{:S(2)}) async-start(), calls=%async_computation.3 | async-start | bytes 3932160
  8.8 3.0 %copy-start.1 = (f32[24,12,256]{2,0,1:T(8,128)}, f32[24,12,256]{2,0,1:T(8,128)S(1)}, u32[]{:S(2)}) copy-start(f32[24,12,256]{2,0,1:T(8,128)S(1)} %fusion.32) | copy-start | bytes 884740
  45.7 76.5 %reduce-scatter.9.cloned.1.call-start = ((), (), s32[]{:S(2)}) async-start(), calls=%async_computation.4 | async-start | bytes 2359296
  51.3 30.8 %copy-start.3 = (u32[32]{0:T(128)S(1)}, u32[32]{0:T(128)}, u32[]{:S(2)}) copy-start(u32[32]{0:T(128)} %constant.19) | copy-start | bytes 388
  51.3 59.5 %copy-start = (bf16[6144,32]{0,1:T(8,128)(2,1)S(1)}, bf16[6144,32]{0,1:T(8,128)(2,1)}, u32[]{:S(2)}) copy-start(bf16[6144,32]{0,1:T(8,128)(2,1)} %param.13) | copy-start | bytes 1179652
  51.3 106.8 %copy-start.2 = (f32[4]{0:T(128)S(1)}, f32[4]{0:T(128)}, u32[]{:S(2)}) copy-start(f32[4]{0:T(128)} %param.15) | copy-start | bytes 52
Sparse Core Ops, SparseCore 0:
  9.6 39.7 all-gather.1
  51.7 59.1 reduce-scatter.6
  113.1 9.0 reduce-scatter.8
where the time goes:
time: 166 us; the launch traced here: 165 us
  matrix products  57.2 us (34%)
  waiting for transfers between devices  41.9 us (25%)
  blocking collectives  30.3 us (18%)
  between operations  15.9 us (10%)
  local copies, waits for them, and re-layouts  15.3 us (9%)
  other arithmetic  4.63 us (3%)
    unnamed x5, waiting for transfers between devices  38.2 us
    dot_general x1, matrix products, local(): jnp.einsum('ijbr,ijrp->ibp', left_tiles, forward_coefs, preferred_element...  29.1 us
    dot_general x1, matrix products, local(): jnp.einsum('ijbr,ijrp->jbp', right_tiles, backward_coefs, preferred_eleme...  28 us
    psum x1, blocking collectives, local(): trace_total = lax.psum(local_trace, ('row', 'col'))  17.8 us
    unnamed x16, local copies, waits for them, and re-layouts  10.2 us
    unnamed x1, blocking collectives  9.82 us
    all_gather x1, waiting for transfers between devices, local(): solved_wide = lax.all_gather(solved_probes, 'col', axis=1, tiled=True)  3.65 us
  transfers between devices with their start and end apart: 3, of which 3 were waited for; matrix products, arithmetic and copies ran while one was open for 42% of the time, Pallas kernels for 0%

commit v1 on v0

v1 whole, which is shorter than its diff:
```python
import functools

import jax
import jax.numpy as jnp
from jax import lax
from jax.experimental import pallas as pl
from jax.experimental.pallas import tpu as pltpu
from jax.sharding import PartitionSpec as P

step_rate = 0.5
MESH = pl.DeviceIdType.MESH
F32 = jnp.float32
BF16 = jnp.bfloat16


def nn(a, b):
    return lax.dot_general(a, b, (((1,), (0,)), ((), ())), preferred_element_type=F32)


def nt(a, b):
    return lax.dot_general(a, b, (((1,), (1,)), ((), ())), preferred_element_type=F32)


def kernel(
    cfg,
    left_hbm,
    right_hbm,
    adm_ref,
    rank_ref,
    probe_ref,
    solved_ref,
    data_ref,
    logp_ref,
    fwd_ref,
    bwd_ref,
    newp_ref,
    left_buf,
    right_buf,
    probe_all,
    solved_all,
    part_f32,
    part_b16,
    fwd_in,
    back_acc,
    back_b16,
    back_in,
    tr_own,
    tr_row,
    tr_col,
    grad_all,
    tile_sem,
    p_sem,
    s1_sem,
    s2_sem,
    f_sem,
    b_sem,
    t_sem,
):
    nh, nr, nc, rows, cols, leaf, cap, lag, depth, slots = cfg
    hyp, row, col = lax.axis_index("hyp"), lax.axis_index("row"), lax.axis_index("col")
    probes = probe_all.shape[0]
    pr, pc = probe_ref.shape[0], solved_ref.shape[0]
    share = solved_ref.shape[1] // nh
    offset = (hyp * rows) // nh

    def row_of(t):
        return lax.rem(t + offset, rows)

    def peer(axis, me, n, d):
        return {axis: lax.rem(me + d, n)}

    def tile_copies(t):
        slot = lax.rem(t, slots)
        i = row_of(t)
        return (
            pltpu.make_async_copy(right_hbm.at[i], right_buf.at[slot], tile_sem.at[0, slot]),
            pltpu.make_async_copy(left_hbm.at[i], left_buf.at[slot], tile_sem.at[1, slot]),
        )

    def start_tiles(t):
        for c in tile_copies(t):
            c.start()

    for t in range(min(depth, rows)):
        start_tiles(t)

    barrier = pltpu.get_barrier_semaphore()
    for axis, me, n in (("row", row, nr), ("col", col, nc), ("hyp", hyp, nh)):
        for d in range(1, n):
            pl.semaphore_signal(barrier, inc=1, device_id=peer(axis, me, n, d), device_id_type=MESH)
    pl.semaphore_wait(barrier, nr + nc + nh - 3)

    def rows_p(r):
        return pl.ds(pl.multiple_of(r * pr, pr), pr)

    def rows_s(c):
        return pl.ds(pl.multiple_of(c * pc, pc), pc)

    def share_of(h):
        return pl.ds(pl.multiple_of(h * share, share), share)

    def remote(src, dst, sems, idx, device):
        return pltpu.make_async_remote_copy(
            src_ref=src,
            dst_ref=dst,
            send_sem=sems.at[(0,) + idx],
            recv_sem=sems.at[(1,) + idx],
            device_id=device,
            device_id_type=MESH,
        )

    p_copies = [
        remote(probe_ref, probe_all.at[rows_p(row)], p_sem, (d - 1,), peer("row", row, nr, d))
        for d in range(1, nr)
    ]
    for c in p_copies:
        c.start()
    s1_copies = [
        remote(
            solved_ref.at[:, share_of(hyp)],
            solved_all.at[rows_s(col), share_of(hyp)],
            s1_sem,
            (d - 1,),
            peer("col", col, nc, d),
        )
        for d in range(1, nc)
    ]
    for c in s1_copies:
        c.start()
    s2_copies = []
    for d in range(1, nc):
        src = solved_all.at[rows_s(lax.rem(col + nc - d, nc)), share_of(hyp)]
        for e in range(1, nh):
            s2_copies.append((d, remote(src, src, s2_sem, (d - 1, e - 1), peer("hyp", hyp, nh, e))))

    probe_all[rows_p(row), :] = probe_ref[...]
    solved_all[rows_s(col), :] = solved_ref[...]

    def zero(j, carry):
        back_acc[j] = jnp.zeros((probes, leaf), F32)
        return carry

    lax.fori_loop(0, cols, zero, 0)

    for c in p_copies:
        c.wait()

    lane = lax.broadcasted_iota(jnp.int32, (1, cap), 1)

    def keep(i, j, values):
        used = jnp.where(adm_ref[i, j] == 0, cap, rank_ref[i, j])
        return jnp.where(lane < used, values, 0.0).astype(BF16)

    def fwd_tile(slot, i, j, acc):
        coef = keep(i, j, nn(probe_all[:, j * leaf : (j + 1) * leaf], right_buf[slot, j]))
        return acc + nt(coef, left_buf[slot, j])

    def bwd_tile(slot, i, j, solved):
        coef = keep(i, j, nn(solved, left_buf[slot, j]))
        back_acc[j] += nt(coef, right_buf[slot, j])

    def send_part(i):
        return [
            remote(
                part_b16.at[i, rows_s(lax.rem(col + d, nc))],
                fwd_in.at[d - 1, i],
                f_sem,
                (d - 1,),
                peer("col", col, nc, d),
            )
            for d in range(1, nc)
        ]

    def step(t, fwd, bwd):
        if fwd:
            for c in tile_copies(t):
                c.wait()
            i, slot = row_of(t), lax.rem(t, slots)
            acc = jnp.zeros((probes, leaf), F32)
        if bwd:
            ib, slotb = row_of(t - lag), lax.rem(t - lag, slots)
            solved = solved_all[:, pl.ds(pl.multiple_of(ib * leaf, leaf), leaf)]
        for j in range(cols):
            if fwd:
                acc = fwd_tile(slot, i, j, acc)
            if bwd:
                bwd_tile(slotb, ib, j, solved)
        if fwd:
            part_f32[i] = acc
            part_b16[i] = acc.astype(BF16)
            for c in send_part(i):
                c.start()

    def run(lo, hi, fwd, bwd, fetch):
        def body(t, carry):
            step(t, fwd, bwd)
            if fetch:
                start_tiles(t + depth)
            return carry

        if hi > lo:
            lax.fori_loop(lo, hi, body, 0)

    early = max(lag - 2, 0)
    last_fetch = rows - depth
    run(0, min(early, last_fetch), True, False, True)
    run(min(early, last_fetch), early, True, False, False)
    for d in range(1, nc):
        s1_copies[d - 1].wait_recv()
        for dd, c in s2_copies:
            if dd == d:
                c.start()
    run(early, min(lag, last_fetch), True, False, True)
    run(max(early, min(lag, last_fetch)), lag, True, False, False)
    own = rows // nh if rows % nh == 0 else 0
    mid = min(lag + own, rows)
    run(lag, min(mid, last_fetch), True, True, True)
    run(max(lag, min(mid, last_fetch)), mid, True, True, False)
    for d, c in s2_copies:
        c.wait_recv()
    run(mid, max(mid, last_fetch), True, True, True)
    run(max(mid, last_fetch), rows, True, True, False)

    def trace_row(i, acc):
        s = solved_all[:, pl.ds(pl.multiple_of(i * leaf, leaf), leaf)].astype(F32)
        return acc + s * part_f32[i]

    def total(x):
        return jnp.full((8, 128), jnp.sum(x), F32)

    tr_own[0] = total(lax.fori_loop(0, rows, trace_row, jnp.zeros((probes, leaf), F32)))
    tr_copies = [
        [
            remote(tr_own.at[0], tr_row.at[d - 1], t_sem, (0, d - 1), peer("row", row, nr, d))
            for d in range(1, nr)
        ],
        [
            remote(tr_own.at[1], tr_col.at[d - 1], t_sem, (1, d - 1), peer("col", col, nc, d))
            for d in range(1, nc)
        ],
        [
            remote(tr_own.at[2], grad_all.at[d], t_sem, (2, d - 1), peer("hyp", hyp, nh, d))
            for d in range(1, nh)
        ],
    ]
    for c in tr_copies[0]:
        c.start()
    cut = [rows + lag * k // 4 for k in range(5)]
    run(cut[0], cut[1], False, True, False)
    for c in tr_copies[0]:
        c.wait()
    value = tr_own[0]
    for d in range(nr - 1):
        value = value + tr_row[d]
    tr_own[1] = value
    for c in tr_copies[1]:
        c.start()
    run(cut[1], cut[2], False, True, False)
    for c in tr_copies[1]:
        c.wait()
    value = tr_own[1]
    for d in range(nc - 1):
        value = value + tr_col[d]
    tr_own[2] = 0.5 * (data_ref[0] - value / probes)
    for c in tr_copies[2]:
        c.start()
    run(cut[2], cut[4], False, True, False)

    def narrow(j, carry):
        back_b16[j] = back_acc[j].astype(BF16)
        return carry

    lax.fori_loop(0, cols, narrow, 0)
    b_copies = [
        remote(
            back_b16.at[:, rows_p(lax.rem(row + d, nr))],
            back_in.at[d - 1],
            b_sem,
            (d - 1,),
            peer("row", row, nr, d),
        )
        for d in range(1, nr)
    ]
    for c in b_copies:
        c.start()

    for d in range(1, nc):
        whole = fwd_in.at[d - 1]
        pltpu.make_async_copy(whole, whole, f_sem.at[0, d - 1]).wait()
        pltpu.make_async_copy(whole, whole, f_sem.at[1, d - 1]).wait()

    def fwd_out(i, carry):
        value = part_f32[i, rows_s(col), :]
        for d in range(nc - 1):
            value = value + fwd_in[d, i].astype(F32)
        fwd_ref[:, pl.ds(pl.multiple_of(i * leaf, leaf), leaf)] = value.astype(BF16)
        return carry

    lax.fori_loop(0, rows, fwd_out, 0)

    for c in tr_copies[2]:
        c.wait()
    grads = [tr_own[2]] + [grad_all[d] for d in range(1, nh)]
    square = grads[0] * grads[0]
    for g in grads[1:]:
        square = square + g * g
    norm = jnp.sqrt(square)
    for d, g in enumerate(grads):
        j = lax.rem(hyp + nh - d, nh)
        newp_ref[j] = logp_ref[j] - (step_rate * g / norm)[0, 0]

    for c in b_copies:
        c.wait()
    for j in range(cols):
        value = back_acc[j, rows_p(row), :]
        for d in range(nr - 1):
            value = value + back_in[d, j].astype(F32)
        bwd_ref[:, j * leaf : (j + 1) * leaf] = value.astype(BF16)

    for c in s1_copies:
        c.wait_send()
    for _, c in s2_copies:
        c.wait_send()


def local(
    sizes,
    left_factors,
    right_factors,
    admissible,
    tile_ranks,
    probes,
    solved_probes,
    data_terms,
    log_params,
):
    nh, nr, nc = sizes
    left, right = left_factors[0], right_factors[0]
    rows, cols, leaf, cap = left.shape
    probe_t, solved_t = probes.T, solved_probes.T
    pr, pc = probe_t.shape[0], solved_t.shape[0]
    count = pr * nr
    row_bytes = 2 * cols * leaf * cap * left.dtype.itemsize
    depth = min(4, rows)
    lag = min(rows // 2, max(1, (44 << 20) // row_bytes - depth))
    slots = lag + depth
    cfg = (nh, nr, nc, rows, cols, leaf, cap, lag, depth, slots)
    vmem = pl.BlockSpec(memory_space=pltpu.VMEM)
    smem = pl.BlockSpec(memory_space=pltpu.SMEM)
    hbm = pl.BlockSpec(memory_space=pl.ANY)
    dma = pltpu.SemaphoreType.DMA
    fwd, bwd, newp = pl.pallas_call(
        functools.partial(kernel, cfg),
        out_shape=(
            jax.ShapeDtypeStruct((pc, rows * leaf), BF16),
            jax.ShapeDtypeStruct((pr, cols * leaf), BF16),
            jax.ShapeDtypeStruct((nh,), F32),
        ),
        in_specs=[hbm, hbm, smem, smem, vmem, vmem, smem, smem],
        out_specs=(vmem, vmem, smem),
        scratch_shapes=[
            pltpu.VMEM((slots, cols, leaf, cap), BF16),
            pltpu.VMEM((slots, cols, leaf, cap), BF16),
            pltpu.VMEM((count, cols * leaf), BF16),
            pltpu.VMEM((count, rows * leaf), BF16),
            pltpu.VMEM((rows, count, leaf), F32),
            pltpu.VMEM((rows, count, leaf), BF16),
            pltpu.VMEM((nc - 1, rows, pc, leaf), BF16),
            pltpu.VMEM((cols, count, leaf), F32),
            pltpu.VMEM((cols, count, leaf), BF16),
            pltpu.VMEM((nr - 1, cols, pr, leaf), BF16),
            pltpu.VMEM((3, 8, 128), F32),
            pltpu.VMEM((nr - 1, 8, 128), F32),
            pltpu.VMEM((nc - 1, 8, 128), F32),
            pltpu.VMEM((nh, 8, 128), F32),
            dma((2, slots)),
            dma((2, nr - 1)),
            dma((2, nc - 1)),
            dma((2, nc - 1, nh - 1)),
            dma((2, nc - 1)),
            dma((2, nr - 1)),
            dma((2, 3, max(nr, nc, nh) - 1)),
        ],
        compiler_params=pltpu.CompilerParams(
            collective_id=0, has_side_effects=True, vmem_limit_bytes=63 << 20
        ),
        cost_estimate=pl.CostEstimate(
            flops=8 * rows * cols * leaf * cap * count,
            bytes_accessed=rows * row_bytes,
            transcendentals=0,
        ),
    )(left, right, admissible, tile_ranks[0], probe_t, solved_t, data_terms, log_params)
    return fwd.T[None], bwd.T[None], newp


def solution(mesh):
    sizes = (mesh.shape["hyp"], mesh.shape["row"], mesh.shape["col"])
    return jax.shard_map(
        functools.partial(local, sizes),
        mesh=mesh,
        in_specs=(
            P("hyp", "row", "col", None, None),
            P("hyp", "row", "col", None, None),
            P("row", "col"),
            P("hyp", "row", "col"),
            P("col", "row"),
            P("row", "col"),
            P("hyp"),
            P(),
        ),
        out_specs=(P("hyp", "row", "col"), P("hyp", "col", "row"), P()),
        check_vma=False,
    )
```

time: 166 us -> 79.1 us (0.48)
  Pallas kernels: 0 us -> 70.1 us
  matrix products: 57.2 us -> 0 us
  waiting for transfers between devices: 41.9 us -> 0 us
  blocking collectives: 30.3 us -> 0 us
  between operations: 15.9 us -> 1.29 us
  local copies, waits for them, and re-layouts: 15.3 us -> 7.36 us
  other arithmetic: 4.63 us -> 0 us
    pallas_call x0 -> x1, Pallas kernels: none -> 70.1 us  [local(): pl.pallas_call(functools.partial(kernel, cfg), out_shape=(jax.ShapeDtypeS...]
    dot_general x2 -> x0, matrix products: 57.2 us -> none  [the longest x1 29.1 us: local(): jnp.einsum('ijbr,ijrp->ibp', left_tiles, forward_coefs, preferred_element...]
    unnamed x5 -> x0, waiting for transfers between devices: 38.2 us -> none
    psum x1 -> x0, blocking collectives: 17.8 us -> none  [local(): trace_total = lax.psum(local_trace, ('row', 'col'))]
    unnamed x1 -> x0, blocking collectives: 9.82 us -> none
    all_gather x1 -> x0, waiting for transfers between devices: 3.65 us -> none  [local(): solved_wide = lax.all_gather(solved_probes, 'col', axis=1, tiled=True)]
    dot_general x2 -> x0, local copies, waits for them, and re-layouts: 2.83 us -> none  [the longest x1 2.38 us: local(): jnp.einsum('ijbr,ijrp->ibp', left_tiles, forward_coefs, preferred_element...]
    unnamed x16 -> x5, local copies, waits for them, and re-layouts: 10.2 us -> 7.36 us
  transfers between devices with their start and end apart: 3 -> 0, of which waited for: 3 -> 0; matrix products, arithmetic and copies ran while one was open for 42% -> 0% of each run, Pallas kernels for 0% -> 0%
where the time goes in v1:
time: 79.1 us; the launch traced here: 78.8 us
  Pallas kernels  70.1 us (89%)
  local copies, waits for them, and re-layouts  7.36 us (9%)
  between operations  1.29 us (2%)
    pallas_call x1, Pallas kernels, local(): pl.pallas_call(functools.partial(kernel, cfg), out_shape=(jax.ShapeDtypeS...  70.1 us
    unnamed x5, local copies, waits for them, and re-layouts  7.36 us

profile of v1, /device:TPU:0, one launch (start us, length us, event | category | flops | bytes accessed | tf_op | source)
XLA Modules:
  0.0 78.8 jit_solution(12024904765608533057)
XLA Ops:
  1.3 1.4 %copy.12.adm_ref = s32[24,12]{1,0:T(8,128)} copy(s32[24,12]{0,1:T(8,128)} %param.10) | data formatting | bytes 2304 | tf_op args[2]
  2.6 1.4 %copy.11 = s32[1,24,12]{2,1,0:T(8,128)} copy(s32[1,24,12]{1,0,2:T(1,128)} %param.11) | data formatting | bytes 2304 | tf_op args[3]
  4.0 70.1 %shard_map.103 = (bf16[32,6144]{1,0:T(8,128)(2,1)}, bf16[64,3072]{1,0:T(8,128)(2,1)}, f32[4]{0:T(128)}) custom-call(bf16[24,12,256,256]{3,2,1,0:T(8,128)(2,1)} %bitcast.11, bf16[24,12,256,256]{3,2,1,0:T(8,128)(2,1)} %bitcast.12, s32[24,12]{1,0:T(8,128)} %copy.12.adm_ref, s32[24,12]{1,0:T(8,128)} %bitcast.17, bf16[64,3072]{1,0:T(8,128)(2,1)} %bitcast.13, ...), custom_call_target="tpu_custom_call" | custom-call | flops 19327352832 | bytes 75497472 | tf_op jit(solution)/shard_map/pallas_call | solution.py:352
  74.2 1.8 %copy.17 = bf16[1,6144,32]{1,2,0:T(8,128)(2,1)} copy(bf16[1,6144,32]{1,2,0:T(8,128)(2,1)} %bitcast.16) | data formatting | bytes 786432
  75.9 1.8 %copy.18 = bf16[1,3072,64]{1,2,0:T(8,128)(2,1)} copy(bf16[1,3072,64]{1,2,0:T(8,128)(2,1)} %bitcast.15) | data formatting | bytes 786432
  77.7 1.1 %copy.19 = f32[4]{0:T(128)} copy(f32[4]{0:T(128)} %get-tuple-element.14) | data formatting | bytes 32

commit v2 on v1

--- a/solution.py
+++ b/solution.py
@@ -151,13 +151,7 @@
         used = jnp.where(adm_ref[i, j] == 0, cap, rank_ref[i, j])
         return jnp.where(lane < used, values, 0.0).astype(BF16)
 
-    def fwd_tile(slot, i, j, acc):
-        coef = keep(i, j, nn(probe_all[:, j * leaf : (j + 1) * leaf], right_buf[slot, j]))
-        return acc + nt(coef, left_buf[slot, j])
-
-    def bwd_tile(slot, i, j, solved):
-        coef = keep(i, j, nn(solved, left_buf[slot, j]))
-        back_acc[j] += nt(coef, right_buf[slot, j])
+    group = max(k for k in range(1, 5) if cols % k == 0)
 
     def send_part(i):
         return [
@@ -180,11 +174,26 @@
         if bwd:
             ib, slotb = row_of(t - lag), lax.rem(t - lag, slots)
             solved = solved_all[:, pl.ds(pl.multiple_of(ib * leaf, leaf), leaf)]
-        for j in range(cols):
-            if fwd:
-                acc = fwd_tile(slot, i, j, acc)
-            if bwd:
-                bwd_tile(slotb, ib, j, solved)
+        held = None
+        for g in range(0, cols + group, group):
+            made = None
+            if g < cols:
+                made = ([], [])
+                for j in range(g, g + group):
+                    if fwd:
+                        wide = nn(probe_all[:, j * leaf : (j + 1) * leaf], right_buf[slot, j])
+                        made[0].append(keep(i, j, wide))
+                    if bwd:
+                        made[1].append(keep(ib, j, nn(solved, left_buf[slotb, j])))
+            if held is not None:
+                js = range(g - group, g)
+                if fwd:
+                    tiles = jnp.concatenate([left_buf[slot, j] for j in js], 1)
+                    acc = acc + nt(jnp.concatenate(held[0], 1), tiles)
+                if bwd:
+                    for k, j in enumerate(js):
+                        back_acc[j] += nt(held[1][k], right_buf[slotb, j])
+            held = made
         if fwd:
             part_f32[i] = acc
             part_b16[i] = acc.astype(BF16)

time: 79.1 us -> 68.8 us (0.87)
  Pallas kernels: 70.1 us -> 59.8 us
    pallas_call x1, Pallas kernels: 70.1 us -> 59.8 us  [local(): pl.pallas_call(functools.partial(kernel, cfg), out_shape=(jax.ShapeDtypeS...]
where the time goes in v2:
time: 68.8 us; the launch traced here: 68.5 us
  Pallas kernels  59.8 us (87%)
  local copies, waits for them, and re-layouts  7.36 us (11%)
  between operations  1.29 us (2%)
    pallas_call x1, Pallas kernels, local(): pl.pallas_call(functools.partial(kernel, cfg), out_shape=(jax.ShapeDtypeS...  59.8 us
    unnamed x5, local copies, waits for them, and re-layouts  7.36 us

profile of v2, /device:TPU:0, one launch (start us, length us, event | category | flops | bytes accessed | tf_op | source)
XLA Modules:
  0.0 68.5 jit_solution(2123350987521539271)
XLA Ops:
  1.3 1.4 %copy.12.adm_ref = s32[24,12]{1,0:T(8,128)} copy(s32[24,12]{0,1:T(8,128)} %param.10) | data formatting | bytes 2304 | tf_op args[2]
  2.6 1.4 %copy.11 = s32[1,24,12]{2,1,0:T(8,128)} copy(s32[1,24,12]{1,0,2:T(1,128)} %param.11) | data formatting | bytes 2304 | tf_op args[3]
  4.0 59.8 %shard_map.103 = (bf16[32,6144]{1,0:T(8,128)(2,1)}, bf16[64,3072]{1,0:T(8,128)(2,1)}, f32[4]{0:T(128)}) custom-call(bf16[24,12,256,256]{3,2,1,0:T(8,128)(2,1)} %bitcast.11, bf16[24,12,256,256]{3,2,1,0:T(8,128)(2,1)} %bitcast.12, s32[24,12]{1,0:T(8,128)} %copy.12.adm_ref, s32[24,12]{1,0:T(8,128)} %bitcast.17, bf16[64,3072]{1,0:T(8,128)(2,1)} %bitcast.13, ...), custom_call_target="tpu_custom_call" | custom-call | flops 19327352832 | bytes 75497472 | tf_op jit(solution)/shard_map/pallas_call | solution.py:361
  63.8 1.8 %copy.17 = bf16[1,6144,32]{1,2,0:T(8,128)(2,1)} copy(bf16[1,6144,32]{1,2,0:T(8,128)(2,1)} %bitcast.16) | data formatting | bytes 786432
  65.6 1.8 %copy.18 = bf16[1,3072,64]{1,2,0:T(8,128)(2,1)} copy(bf16[1,3072,64]{1,2,0:T(8,128)(2,1)} %bitcast.15) | data formatting | bytes 786432
  67.4 1.1 %copy.19 = f32[4]{0:T(128)} copy(f32[4]{0:T(128)} %get-tuple-element.14) | data formatting | bytes 32
